TPU v7x, 512 devices: a whole 4x4x16 slice. The times are simulated.
512 devices in a mesh: segment: 4 (over y), seq: 16 (over z), head: 8 (over x, core).
Axes of the slice: x: 4, y: 4, z: 16, core: 2. Of those that a mesh axis runs over, the one named last changes fastest.
Arguments:
- queries: bfloat16 [8192, 8192], P(('segment', 'seq', 'head')), may hold values from -38 to 38
- span_keys: bfloat16 [8192, 1024], P(('segment', 'seq', 'head')), may hold values from -4 to 4
- span_values: bfloat16 [8192, 1024], P(('segment', 'seq', 'head')), may hold values from -4 to 4
- cache_keys: bfloat16 [128, 128, 8, 128], P('seq', None, 'head'), may hold values from -4 to 4
- cache_values: bfloat16 [128, 128, 8, 128], P('seq', None, 'head'), may hold values from -4 to 4
- hit_holder: int32 [128], replicated, may hold values from 0 to 15, as said below
- hit_slot: int32 [128], replicated, may hold values from 0 to 7
- sparse_lists: int32 [64, 8, 8], replicated, may hold values from 0 to 127, as said below
Outputs:
- attended: bfloat16 [8192, 8192], P(('segment', 'seq'), 'head')
Inputs may be any that keep to these rules, and one draw needn't show every extreme that they name: hit_holder and hit_slot together name every pair of holder and slot exactly once, so each holder keeps 8 prefix blocks. `sparse_lists`: A list names 8 different blocks; they are kept by exactly 8 different holders, 1 block from each.
All inputs are finite; a program needn't handle non-finite values.
Results may differ from a plain program's by a relative error of at most 0.0049.
Values may be sent and summed in bfloat16 or wider, within the bound.
A program may use at most 64 MiB of HBM per device.

v0:
```python
import math

import jax
import jax.numpy as jnp
from jax import lax
from jax.sharding import PartitionSpec as P

HD = 128
BLK = 128
SEL = 8
HOLD_BLK = 8
QPG = 8


def lookup(table_values, index_values):
    id_range = jnp.arange(table_values.shape[0], dtype=jnp.int32)
    return jnp.sum(jnp.where(index_values[..., None] == id_range, table_values, 0), axis=-1)


def soft_step(row_peak, row_total, scores, valid):
    if valid is not None:
        scores = jnp.where(valid, scores, -1e30)
    new_peak = jnp.maximum(row_peak, jnp.max(scores, axis=-1))
    weight = jnp.exp(scores - new_peak[..., None])
    if valid is not None:
        weight = jnp.where(valid, weight, 0.0)
    shrink = jnp.exp(row_peak - new_peak)
    return (new_peak, shrink, weight, row_total * shrink + jnp.sum(weight, axis=-1))


def local(
    queries, span_keys, span_values, cache_keys, cache_values, hit_holder, hit_slot, sparse_lists
):
    q_local, k_local, v_local = (
        lax.all_to_all(queries, "head", split_axis=1, concat_axis=0, tiled=True),
        lax.all_to_all(span_keys, "head", split_axis=1, concat_axis=0, tiled=True),
        lax.all_to_all(span_values, "head", split_axis=1, concat_axis=0, tiled=True),
    )
    row_count = q_local.shape[0]
    kv_local = k_local.shape[1] // HD
    blocks_dev = row_count // BLK
    head_idx = lax.axis_index("head")
    row_base = lax.axis_index(("segment", "seq")) * row_count
    score_scale = HD ** (-0.5)
    chosen = lax.dynamic_slice(
        sparse_lists,
        (lax.axis_index(("segment", "seq")) * blocks_dev, head_idx * kv_local, 0),
        (blocks_dev, kv_local, SEL),
    )
    kv_ids = jnp.arange(kv_local, dtype=jnp.int32)
    wanted = jnp.transpose(lookup(hit_holder * HOLD_BLK + hit_slot, chosen), (1, 0, 2))
    heads_col = kv_ids[:, None, None]
    zero_blocks = jnp.zeros((kv_local, blocks_dev, SEL, BLK, HD), jnp.bfloat16)
    running = (zero_blocks, zero_blocks)
    portion_k = lax.all_gather(cache_keys, "seq", axis=0, tiled=True)
    portion_v = lax.all_gather(cache_values, "seq", axis=0, tiled=True)
    key_count = portion_k.shape[0]
    inside = ((wanted >= 0) & (wanted < key_count))[..., None, None]
    safe_index = jnp.clip(wanted, 0, key_count - 1)
    new_k = jnp.where(inside, portion_k[safe_index, :, heads_col, :], running[0])
    new_v = jnp.where(inside, portion_v[safe_index, :, heads_col, :], running[1])
    q_blocks = q_local.reshape(blocks_dev, BLK, kv_local, QPG, HD)
    key_rows = new_k.reshape(kv_local, blocks_dev, SEL * BLK, HD)
    value_rows = new_v.reshape(kv_local, blocks_dev, SEL * BLK, HD)
    prefix_scores = (
        jnp.einsum("atgpd,gakd->gatpk", q_blocks, key_rows, preferred_element_type=jnp.float32)
        * score_scale
    )
    prefix_scores = prefix_scores.reshape(kv_local, row_count, QPG, SEL * BLK)
    start_peak = jnp.full((kv_local, row_count, QPG), -1e30, jnp.float32)
    start_total = jnp.zeros((kv_local, row_count, QPG), jnp.float32)
    row_peak, shrink, weight, row_total = soft_step(start_peak, start_total, prefix_scores, None)
    weight_blocks = weight.astype(jnp.bfloat16).reshape(kv_local, blocks_dev, BLK, QPG, SEL * BLK)
    weighted = jnp.einsum(
        "gatpk,gakd->gatpd", weight_blocks, value_rows, preferred_element_type=jnp.float32
    )
    weighted = weighted.reshape(kv_local, row_count, QPG, HD)
    q_rows = q_local.reshape(row_count, kv_local, QPG, HD)
    query_pos = row_base + jnp.arange(row_count, dtype=jnp.int32)

    def attend(online, key_part, value_part, key_start):
        key_count = key_part.shape[0]
        scores = (
            jnp.einsum("rgpd,kgd->grpk", q_rows, key_part, preferred_element_type=jnp.float32)
            * score_scale
        )
        valid = (key_start + jnp.arange(key_count, dtype=jnp.int32))[
            None, None, None, :
        ] <= query_pos[None, :, None, None]
        new_peak, shrink_now, weight_now, new_total = soft_step(online[0], online[1], scores, valid)
        mixed = jnp.einsum(
            "grpk,kgd->grpd",
            weight_now.astype(jnp.bfloat16),
            value_part,
            preferred_element_type=jnp.float32,
        )
        return (new_peak, new_total, online[2] * shrink_now[..., None] + mixed)

    online = (row_peak, row_total, weighted)
    portion_k = lax.all_gather(k_local, ("segment", "seq"), axis=0, tiled=True)
    portion_v = lax.all_gather(v_local, ("segment", "seq"), axis=0, tiled=True)
    key_count = portion_k.shape[0]
    block_size = math.gcd(key_count, 512)
    part_count = key_count // block_size
    key_blocks = portion_k.reshape(part_count, block_size, kv_local, HD)
    value_blocks = portion_v.reshape(part_count, block_size, kv_local, HD)
    block_starts = jnp.arange(part_count, dtype=jnp.int32) * block_size

    def inner(running, block_items):
        key_part, value_part, key_start = block_items
        running = attend(running, key_part, value_part, key_start)
        return (running, None)

    online, _ = lax.scan(inner, online, (key_blocks, value_blocks, block_starts))
    row_peak, row_total, weighted = online
    result = (weighted / row_total[..., None]).astype(jnp.bfloat16)
    return jnp.transpose(result, (1, 0, 2, 3)).reshape(row_count, kv_local * QPG * HD)


def solution(mesh):
    placed = (
        P(("segment", "seq", "head"), None),
        P(("segment", "seq", "head"), None),
        P(("segment", "seq", "head"), None),
        P("seq", None, "head", None),
        P("seq", None, "head", None),
        P(),
        P(),
        P(),
    )
    return jax.shard_map(
        local, mesh=mesh, in_specs=placed, out_specs=P(("segment", "seq"), "head"), check_vma=False
    )
```

profile of v0, /device:TPU:1, one launch (start us, length us, event | category | flops | bytes accessed | tf_op | source)
XLA Modules:
  0.0 531.5 jit_solution(5961568287807678471)
XLA Ops:
  8.1 14.6 %all_to_all.54 = bf16[16,8,128]{2,0,1:T(8,128)(2,1)} all-to-all(bf16[16,8,128]{2,0,1:T(8,128)(2,1)S(1)} %copy_bitcast_fusion.3), channel_id=1, replica_groups=mesh['segment'=4,'seq'=16,'head'=8] {'head'}, dimensions={1} | all-to-all | bytes 65536 | tf_op jit(solution)/shard_map/all_to_all | solution.py:36
  23.6 8.5 %all_to_all.55 = bf16[16,8,128]{2,0,1:T(8,128)(2,1)} all-to-all(bf16[16,8,128]{2,0,1:T(8,128)(2,1)S(1)} %copy_bitcast_fusion.2), channel_id=1, replica_groups=mesh['segment'=4,'seq'=16,'head'=8] {'head'}, dimensions={1} | all-to-all | bytes 65536 | tf_op jit(solution)/shard_map/all_to_all | solution.py:37
  33.7 4.0 all-to-all-start
  39.7 4.7 all-to-all-done
  44.5 40.2 %all-gather.5.cloned.1.call-done = bf16[128,128,1,128]{3,1,2,0:T(8,128)(2,1)} async-done(((bf16[8,128,1,128]{3,1,2,0:T(8,128)(2,1)}), bf16[128,128,1,128]{3,1,2,0:T(8,128)(2,1)}) %all-gather.5.cloned.1.call-update) | async-done | bytes 4194320 | tf_op jit(solution)/shard_map/all_gather | solution.py:55
  84.7 2.8 gather_fusion
  87.5 74.6 %all-gather.7.cloned.1.call-done = bf16[128,128,1,128]{3,1,2,0:T(8,128)(2,1)} async-done(((bf16[8,128,1,128]{3,1,2,0:T(8,128)(2,1)}), bf16[128,128,1,128]{3,1,2,0:T(8,128)(2,1)}) %all-gather.7.cloned.1.call-update) | async-done | bytes 4194320 | tf_op jit(solution)/shard_map/all_gather | solution.py:56
  162.1 2.8 gather_fusion.1
  167.5 135.1 %all-gather.9.cloned.1.call-done = bf16[8192,128]{1,0:T(8,128)(2,1)} async-done(((bf16[128,128]{1,0:T(8,128)(2,1)}), bf16[8192,128]{1,0:T(8,128)(2,1)}) %all-gather.9.cloned.1.call-update) | async-done | bytes 2097168 | tf_op jit(solution)/shard_map/all_gather | solution.py:100
  302.6 139.8 %all-gather.11.cloned.1.call-done = bf16[8192,128]{1,0:T(8,128)(2,1)} async-done(((bf16[128,128]{1,0:T(8,128)(2,1)}), bf16[8192,128]{1,0:T(8,128)(2,1)}) %all-gather.11.cloned.1.call-update) | async-done | bytes 2097168 | tf_op jit(solution)/shard_map/all_gather | solution.py:101
  442.4 81.5 %while.15 = (s32[]{:T(128)}, f32[1,128,8]{1,2,0:T(8,128)S(1)}, f32[1,128,8]{1,2,0:T(8,128)S(1)}, f32[1,128,8,128]{3,1,2,0:T(8,128)S(1)}, s32[16]{0:T(128)S(1)}, ...) while((s32[]{:T(128)}, f32[1,128,8]{1,2,0:T(8,128)S(1)}, ...), condition=%wide.region_6.7_spmd.clone, body=%wide.region_3.6_spmd.clone.sunk | while | flops 275582592 | bytes 8197257 | solution.py:114
  445.7 1.7 fusion.52
  450.8 1.7 fusion.52
  455.9 1.7 fusion.52
  461.0 1.7 fusion.52
  466.1 1.7 fusion.52
  471.2 1.7 fusion.52
  476.2 1.7 fusion.52
  481.3 1.7 fusion.52
  486.4 1.7 fusion.52
  496.6 1.7 fusion.52
  501.7 1.7 fusion.52
  506.8 1.7 fusion.52
  517.0 1.7 fusion.52
  (181 shorter events, 67.1 us)
Async XLA Ops:
  6.5 1.5 copy-start
  6.5 78.1 %all-gather.5.cloned.1.call-start = ((), (), s32[]{:S(2)}) async-start(), calls=%async_computation.3 | async-start | bytes 4456448 | tf_op jit(solution)/shard_map/all_gather | solution.py:55
  7.3 154.8 %all-gather.7.cloned.1.call-start = ((), (), s32[]{:S(2)}) async-start(), calls=%async_computation.4 | async-start | bytes 4456448 | tf_op jit(solution)/shard_map/all_gather | solution.py:56
  8.0 294.6 %all-gather.9.cloned.1.call-start = ((), (), s32[]{:S(2)}) async-start(), calls=%async_computation.5 | async-start | bytes 2129920 | tf_op jit(solution)/shard_map/all_gather | solution.py:100
  22.7 419.6 %all-gather.11.cloned.1.call-start = ((), (), s32[]{:S(2)}) async-start(), calls=%async_computation.6 | async-start | bytes 2129920 | tf_op jit(solution)/shard_map/all_gather | solution.py:101
  33.7 10.6 %all-to-all-start = ((bf16[16,8,1024]{2,0,1:T(8,128)(2,1)}), bf16[16,8,1024]{2,0,1:T(8,128)(2,1)S(1)}, u32[]{:S(2)}, u32[]{:S(2)}) async-start(bf16[16,8,1024]{2,0,1:T(8,128)(2,1)} %bitcast.115), calls=%async_computation | async-start | bytes 524288 | tf_op jit(solution)/shard_map/all_to_all | solution.py:35
Sparse Core Ops, SparseCore 0:
  9.4 75.1 all-gather.4
  86.8 75.2 all-gather.6
  165.0 137.4 all-gather.8
  305.4 136.9 all-gather.10
where the time goes:
time: 541 us; the launch traced here: 532 us
  waiting for transfers between devices  396 us (73%)
  matrix products  51.2 us (9%)
  other arithmetic  23.2 us (4%)
  blocking collectives  23.1 us (4%)
  local copies, waits for them, and re-layouts  19.4 us (4%)
  between operations  13.3 us (2%)
    all_gather x1, waiting for transfers between devices, local(): portion_v = lax.all_gather(v_local, ('segment', 'seq'), axis=0, tiled=True)  140 us
    all_gather x1, waiting for transfers between devices, local(): portion_k = lax.all_gather(k_local, ('segment', 'seq'), axis=0, tiled=True)  135 us
    all_gather x1, waiting for transfers between devices, local(): portion_v = lax.all_gather(cache_values, 'seq', axis=0, tiled=True)  74.6 us
    all_gather x1, waiting for transfers between devices, local(): portion_k = lax.all_gather(cache_keys, 'seq', axis=0, tiled=True)  40.2 us
    dot_general x16, matrix products, attend(): jnp.einsum('grpk,kgd->grpd', weight_now.astype(jnp.bfloat16), value_part,...  27.9 us
    dot_general x16, matrix products, attend(): jnp.einsum('rgpd,kgd->grpk', q_rows, key_part, preferred_element_type=jnp...  21.8 us
    all_to_all x1, blocking collectives, local(): lax.all_to_all(span_keys, 'head', split_axis=1, concat_axis=0, tiled=True)  14.6 us
  transfers between devices with their start and end apart: 5, of which 5 were waited for; matrix products, arithmetic and copies ran while one was open for 2% of the time, Pallas kernels for 0%

commit v1 on v0

v1 whole, which is shorter than its diff:
```python
import functools

import jax
import jax.numpy as jnp
from jax import lax
from jax.experimental import pallas as pl
from jax.experimental.pallas import tpu as pltpu
from jax.sharding import PartitionSpec as P

HD = 128
BLK = 128
SEL = 8
HOLD_BLK = 8
QPG = 8
LOG2E = 1.4426950408889634
SCALE = HD ** -0.5 * LOG2E
NT = (((1,), (1,)), ((), ()))
NN = (((1,), (0,)), ((), ()))


def wait_bytes(ref, sem):
    pltpu.make_async_copy(ref, ref, sem).wait()


def kernel(
    ny, nz, nh,
    q_in, k_in, v_in, ck, cv, hold, slot, lists, out,
    qb, sk, sv, pk, pv, bias, acc, peak, sendo, recvo, sendl, recvl, kp, vp, lists_s,
    q_send, q_recv, kv_send, kv_recv, ring_send, ring_recv, o_send, o_recv, l_send, l_recv,
    own_sem, list_sem,
):
    y, z, h = lax.axis_index("segment"), lax.axis_index("seq"), lax.axis_index("head")
    plane = ny * nh
    me = y * nh + h
    rows = BLK // nh
    stripe = BLK // ny
    per = nh // ny
    right, left = lax.rem(z + 1, nz), lax.rem(z + nz - 1, nz)
    half = nz // 2

    own_rows = pl.ds(pl.multiple_of(y * stripe, stripe), stripe)
    own_slots = pl.ds(z * HOLD_BLK, HOLD_BLK)
    own_k = pltpu.make_async_copy(ck.at[:, own_rows, :], pk.at[own_slots], own_sem.at[0])
    own_v = pltpu.make_async_copy(cv.at[:, own_rows, :], pv.at[own_slots], own_sem.at[1])
    get_lists = pltpu.make_async_copy(lists.at[h], lists_s, list_sem)

    barrier = pltpu.get_barrier_semaphore()

    def greet(o, _):
        i = lax.rem(me + o, plane)
        pl.semaphore_signal(
            barrier, inc=1, device_id={"segment": lax.div(i, nh), "head": lax.rem(i, nh)}
        )
        return 0

    pl.semaphore_signal(barrier, inc=1, device_id={"seq": left})
    pl.semaphore_signal(barrier, inc=1, device_id={"seq": right})
    lax.fori_loop(1, plane, greet, 0)
    own_k.start()
    own_v.start()
    get_lists.start()
    pl.semaphore_wait(barrier, plane + 1)

    tables = (sk, sv, pk, pv)

    def piece(kind, origin):
        if kind < 2:
            return tables[kind].at[:, origin]
        return tables[kind].at[pl.ds(origin * HOLD_BLK, HOLD_BLK)]

    def steps(kind, way):
        return half if kind % 2 == way else half - 1

    def ring_copy(kind, way, step, src, origin):
        return pltpu.make_async_remote_copy(
            src_ref=src,
            dst_ref=piece(kind, origin),
            send_sem=ring_send.at[kind * 2 + way, step],
            recv_sem=ring_recv.at[kind * 2 + way, step],
            device_id={"seq": left if way else right},
        )

    def origin_at(way, step):
        return lax.rem(z + step, nz) if way else lax.rem(z + nz - step, nz)

    def relay(kind, way, step):
        origin = origin_at(way, step)
        last = steps(kind, way)

        def go():
            wait_bytes(piece(kind, origin), ring_recv.at[kind * 2 + way, step - 1])

        def send():
            ring_copy(kind, way, step, piece(kind, origin), origin).start()

        if isinstance(step, int):
            if step <= last:
                go()
            if step < last:
                send()
        else:
            pl.when(step <= last)(go)
            pl.when(step < last)(send)

    for way in (0, 1):
        for kind, src in ((2, ck), (3, cv)):
            if steps(kind, way) > 0:
                ring_copy(kind, way, 0, src.at[:, own_rows, :], z).start()

    target = lax.div(h, per)
    dst_rows = pl.ds(pl.multiple_of(lax.rem(h, per) * rows, rows), rows)

    def head_cols(i, width):
        return pl.ds(pl.multiple_of(i * width, width), width)

    def send_kv(o, _):
        i = lax.rem(h + o, nh)
        here = (target == y) & (i == h)

        def local_copy():
            for n, (src, tab) in enumerate(((k_in, sk), (v_in, sv))):
                pltpu.make_async_copy(
                    src.at[:, head_cols(i, HD)], tab.at[y, z, dst_rows], kv_recv.at[n]
                ).start()

        def remote_copy():
            for n, (src, tab) in enumerate(((k_in, sk), (v_in, sv))):
                pltpu.make_async_remote_copy(
                    src_ref=src.at[:, head_cols(i, HD)],
                    dst_ref=tab.at[y, z, dst_rows],
                    send_sem=kv_send.at[n],
                    recv_sem=kv_recv.at[n],
                    device_id={"segment": target, "head": i},
                ).start()

        pl.when(here)(local_copy)
        pl.when(jnp.logical_not(here))(remote_copy)
        return 0

    lax.fori_loop(0, nh, send_kv, 0)

    pltpu.make_async_copy(q_in.at[:, head_cols(h, QPG * HD)], qb.at[me], q_recv).start()

    def send_q(o, _):
        i = lax.rem(me + o, plane)
        g = lax.rem(i, nh)
        pltpu.make_async_remote_copy(
            src_ref=q_in.at[:, head_cols(g, QPG * HD)],
            dst_ref=qb.at[me],
            send_sem=q_send,
            recv_sem=q_recv,
            device_id={"segment": lax.div(i, nh), "head": g},
        ).start()
        return 0

    lax.fori_loop(1, plane, send_q, 0)

    width = nz * stripe
    row_id = lax.broadcasted_iota(jnp.int32, (BLK, width), 0)
    col_id = lax.broadcasted_iota(jnp.int32, (BLK, width), 1)
    key_pos = lax.div(col_id, stripe) * BLK + lax.rem(col_id, stripe) + y * stripe
    bias[...] = jnp.where(key_pos <= z * BLK + row_id, 0.0, -1e30).astype(jnp.float32)

    for n, tab in enumerate((sk, sv)):
        wait_bytes(tab.at[:, z], kv_recv.at[n])
        for way in (0, 1):
            if steps(n, way) > 0:
                ring_copy(n, way, 0, piece(n, z), z).start()

    def span_step(s, _):
        for kind in (0, 1):
            for way in (0, 1):
                relay(kind, way, s)
        return 0

    lax.fori_loop(1, half + 1, span_step, 0)
    wait_bytes(qb, q_recv)

    def query_pair(yp, pair):
        parts = [
            qb[pl.ds(yp * nh, nh), :, head_cols(pair * 2 + j, HD)].reshape(BLK, HD)
            for j in (0, 1)
        ]
        return jnp.concatenate(parts, axis=0)

    def span_unit(yp, pair):
        n = (yp + 1) * width
        keys = sk[0 : yp + 1].reshape(n, HD)
        values = sv[0 : yp + 1].reshape(n, HD)
        values = jnp.concatenate([values, jnp.ones_like(values)], axis=1)
        s = lax.dot_general(query_pair(yp, pair), keys, NT, preferred_element_type=jnp.float32)
        b = bias[...]
        last = s[:, n - width :] + jnp.concatenate([b, b], axis=0)
        s = jnp.concatenate([s[:, : n - width], last], axis=1) if yp else last
        m = jnp.max(s, axis=1, keepdims=True) * SCALE
        w = jnp.exp2(s * SCALE - m).astype(jnp.bfloat16)
        r = lax.dot_general(w, values, NN, preferred_element_type=jnp.float32)
        m = jnp.broadcast_to(m, (2 * BLK, HD))
        for j in (0, 1):
            acc[yp * QPG + pair * 2 + j] = r[j * BLK : (j + 1) * BLK]
            peak[yp * QPG + pair * 2 + j] = m[j * BLK : (j + 1) * BLK]

    def span_pair(pair, _):
        for part in (0, 1):
            s = 2 * pair + 1 + part
            for kind in (2, 3):
                for way in (0, 1):
                    relay(kind, way, s)
            for yp in range(ny - 1, -1, -1):
                if (yp == ny - 1) == (part == 0):
                    span_unit(yp, pair)
        return 0

    lax.fori_loop(0, QPG // 2, span_pair, 0)

    own_k.wait()
    own_v.wait()
    get_lists.wait()
    lane = lax.broadcasted_iota(jnp.int32, (BLK, HD), 1)

    order = sorted(range(ny), key=lambda o: (o == 0, -min(o, ny - o)))
    for o in order:
        yp = lax.rem(y + o, ny)
        for i in range(SEL):
            block = lists_s[i, yp * nz + z]
            at = hold[block] * HOLD_BLK + slot[block]
            kp[i * stripe : (i + 1) * stripe, :] = pk[at]
            vp[i * stripe : (i + 1) * stripe, :] = pv[at]

        def prefix_pair(pair, level):
            values = vp[...]
            values = jnp.concatenate([values, jnp.ones_like(values)], axis=1)
            s = lax.dot_general(
                query_pair(yp, pair), kp[...], NT, preferred_element_type=jnp.float32
            )
            base = yp * QPG + pair * 2
            m1 = jnp.concatenate([peak[base], peak[base + 1]], axis=0)
            m = jnp.maximum(m1, jnp.max(s, axis=1, keepdims=True) * SCALE)
            mm = jnp.concatenate([m] * (SEL * stripe // HD), axis=1)
            w = jnp.exp2(s * SCALE - mm).astype(jnp.bfloat16)
            r = lax.dot_general(w, values, NN, preferred_element_type=jnp.float32)
            fade = jnp.exp2(m1 - m)
            a = jnp.concatenate([acc[base], acc[base + 1]], axis=0)
            total = a[:, HD:] * fade + r[:, HD:]
            mixed = ((a[:, :HD] * fade + r[:, :HD]) / total).astype(jnp.bfloat16)
            lse = m + jnp.log2(total)
            for j in (0, 1):
                sendo[yp, :, head_cols(pair * 2 + j, HD)] = mixed[j * BLK : (j + 1) * BLK]
                level = jnp.where(lane == pair * 2 + j, lse[j * BLK : (j + 1) * BLK], level)
            if o:
                cols = head_cols(pair, 2 * HD)
                pltpu.make_async_remote_copy(
                    src_ref=sendo.at[yp, :, cols],
                    dst_ref=recvo.at[y, :, cols],
                    send_sem=o_send.at[o],
                    recv_sem=o_recv.at[o],
                    device_id={"segment": yp},
                ).start()
            return level

        level = lax.fori_loop(0, QPG // 2, prefix_pair, jnp.zeros((BLK, HD), jnp.float32))
        sendl[yp] = level.T[:QPG]
        if o:
            pltpu.make_async_remote_copy(
                src_ref=sendl.at[yp],
                dst_ref=recvl.at[y],
                send_sem=l_send.at[o],
                recv_sem=l_recv.at[o],
                device_id={"segment": yp},
            ).start()

    levels = [sendl[y]]
    parts = [sendo.at[y]]
    for o in order[:-1]:
        src = lax.rem(y + ny - o, ny)
        wait_bytes(recvl.at[src], l_recv.at[o])
        wait_bytes(recvo.at[src], o_recv.at[o])
        levels.append(recvl[src])
        parts.append(recvo.at[src])
    top = functools.reduce(jnp.maximum, levels)
    shares = [jnp.exp2(v - top) for v in levels]
    norm = 1.0 / functools.reduce(jnp.add, shares)
    fill = jnp.zeros((BLK - QPG, BLK), jnp.float32)
    shares = [jnp.concatenate([v * norm, fill], axis=0).T for v in shares]
    for p in range(QPG):
        cols = slice(p * HD, (p + 1) * HD)
        out[:, cols] = functools.reduce(
            jnp.add,
            [w[:, p : p + 1] * part[:, cols].astype(jnp.float32) for w, part in zip(shares, parts)],
        ).astype(jnp.bfloat16)

    wait_bytes(qb.at[: plane - 1], q_send)
    for n, src in enumerate((k_in, v_in)):
        pl.when(target == y)(
            functools.partial(wait_bytes, src.at[:, : (nh - 1) * HD], kv_send.at[n])
        )
        pl.when(target != y)(functools.partial(wait_bytes, src, kv_send.at[n]))
    for kind in range(4):
        for way in (0, 1):
            count = steps(kind, way)

            def sent(step, _, kind=kind, way=way):
                wait_bytes(piece(kind, z), ring_send.at[kind * 2 + way, step])
                return 0

            lax.fori_loop(0, count, sent, 0)
    for o in range(1, ny):
        wait_bytes(sendo.at[0], o_send.at[o])
        wait_bytes(sendl.at[0], l_send.at[o])


def local(ny, nz, nh, q, k, v, ck, cv, hold, slot, lists):
    rows, width, stripe = BLK // nh, QPG * HD, BLK // ny
    blocks = ck.shape[0] * nz
    ck = ck.reshape(ck.shape[0], BLK, HD)
    cv = cv.reshape(cv.shape[0], BLK, HD)
    lists = jnp.transpose(lists, (1, 2, 0))
    any_, smem = pl.BlockSpec(memory_space=pl.ANY), pl.BlockSpec(memory_space=pltpu.SMEM)
    bf, f32, dma = jnp.bfloat16, jnp.float32, pltpu.SemaphoreType.DMA
    return pl.pallas_call(
        functools.partial(kernel, ny, nz, nh),
        out_shape=jax.ShapeDtypeStruct((BLK, width), bf),
        in_specs=[any_] * 5 + [smem, smem, any_],
        out_specs=pl.BlockSpec(memory_space=pltpu.VMEM),
        scratch_shapes=[
            pltpu.VMEM((ny * nh, rows, width), bf),
            pltpu.VMEM((ny, nz, stripe, HD), bf),
            pltpu.VMEM((ny, nz, stripe, HD), bf),
            pltpu.VMEM((blocks, stripe, HD), bf),
            pltpu.VMEM((blocks, stripe, HD), bf),
            pltpu.VMEM((BLK, nz * stripe), f32),
            pltpu.VMEM((ny * QPG, BLK, 2 * HD), f32),
            pltpu.VMEM((ny * QPG, BLK, HD), f32),
            pltpu.VMEM((ny, BLK, width), bf),
            pltpu.VMEM((ny, BLK, width), bf),
            pltpu.VMEM((ny, QPG, BLK), f32),
            pltpu.VMEM((ny, QPG, BLK), f32),
            pltpu.VMEM((SEL * stripe, HD), bf),
            pltpu.VMEM((SEL * stripe, HD), bf),
            pltpu.SMEM((SEL, lists.shape[2]), jnp.int32),
            dma, dma, dma((2,)), dma((2,)),
            dma((8, nz // 2)), dma((8, nz // 2)),
            dma((ny,)), dma((ny,)), dma((ny,)), dma((ny,)),
            dma((2,)), dma,
        ],
        compiler_params=pltpu.CompilerParams(
            collective_id=0, has_side_effects=True, vmem_limit_bytes=52 * 2**20
        ),
        cost_estimate=pl.CostEstimate(
            flops=4 * BLK * QPG * HD * 6144, bytes_accessed=2**24, transcendentals=6144 * 1024
        ),
        name="attend",
    )(q, k, v, ck, cv, hold, slot, lists)


def solution(mesh):
    ny, nz, nh = mesh.shape["segment"], mesh.shape["seq"], mesh.shape["head"]
    placed = (
        P(("segment", "seq", "head"), None),
        P(("segment", "seq", "head"), None),
        P(("segment", "seq", "head"), None),
        P("seq", None, "head", None),
        P("seq", None, "head", None),
        P(),
        P(),
        P(),
    )
    return jax.shard_map(
        functools.partial(local, ny, nz, nh),
        mesh=mesh,
        in_specs=placed,
        out_specs=P(("segment", "seq"), "head"),
        check_vma=False,
    )
```

time: 541 us -> 96.1 us (0.18)
  the two profiles are of different devices: /device:TPU:1 before, /device:TPU:34 now
where the time goes in v1:
time: 96.1 us; the launch traced here: 95.7 us
  Pallas kernels  89.2 us (93%)
  local copies, waits for them, and re-layouts  6.5 us (7%)
    pallas_call x1, Pallas kernels, local(): pl.pallas_call(functools.partial(kernel, ny, nz, nh), out_shape=jax.Shape...  89.2 us
    unnamed x17, local copies, waits for them, and re-layouts  6.5 us

profile of v1, /device:TPU:34, one launch (start us, length us, event | category | flops | bytes accessed | tf_op | source)
XLA Modules:
  0.0 95.7 jit_solution(3298655800089427134)
XLA Ops:
  0.0 0.0 copy-start.6
  0.0 0.0 copy-start.7
  0.0 0.7 copy-done.6
  0.7 0.0 copy-done.7
  0.7 0.0 copy-start
  0.7 0.9 copy-done
  1.6 0.0 copy-start.1
  1.6 0.9 copy-done.1
  2.6 0.0 copy-start.2
  2.6 0.9 copy-done.2
  3.5 0.0 copy-start.3
  3.5 0.8 copy-done.3
  4.3 0.0 copy-start.4
  4.3 0.8 copy-done.4
  5.0 0.0 copy-start.5
  5.0 0.8 copy-done.5
  5.8 89.2 %attend.1 = bf16[128,1024]{1,0:T(8,128)(2,1)S(1)} custom-call(bf16[16,8192]{1,0:T(8,128)(2,1)S(1)} %copy-done, bf16[16,1024]{1,0:T(8,128)(2,1)S(1)} %copy-done.3, bf16[16,1024]{1,0:T(8,128)(2,1)S(1)} %copy-done.4, bf16[8,128,128]{2,1,0:T(8,128)(2,1)S(1)} %bitcast.3, bf16[8,128,128]{2,1,0:T(8,128)(2,1)S(1)} %bitcast.4, s32[128]{0:T(128)S(1)} %copy-done.6, ...), custom_call_target="tpu_custom_call" | custom-call | flops 3221225472 | bytes 16777216 | tf_op jit(solution)/shard_map/attend/pallas_call | solution.py:320
  95.0 0.7 copy.10
Async XLA Ops:
  0.0 0.7 copy-start.6
  0.0 0.7 copy-start.7
  0.7 0.9 copy-start
  1.6 0.9 copy-start.1
  2.6 0.9 copy-start.2
  3.5 0.8 copy-start.3
  4.3 0.8 copy-start.4
  5.0 0.8 copy-start.5

commit v2 on v1

v2 whole, which is shorter than its diff:
```python
import functools

import jax
import jax.numpy as jnp
from jax import lax
from jax.experimental import pallas as pl
from jax.experimental.pallas import tpu as pltpu
from jax.sharding import PartitionSpec as P

HD = 128
BLK = 128
SEL = 8
HOLD_BLK = 8
QPG = 8
GROUP = 4
LOG2E = 1.4426950408889634
SCALE = HD ** -0.5 * LOG2E
NT = (((1,), (1,)), ((), ()))
NN = (((1,), (0,)), ((), ()))


def wait_bytes(ref, sem):
    pltpu.make_async_copy(ref, ref, sem).wait()


def kernel(
    ny, nz, nh,
    q_in, k_in, v_in, ck, cv, hold, slot, lists, out,
    qb, sk, sv, pk, pv, kc, vc, bias, acc, peak, sendo, recvo, sendl, recvl, kp, vp, lists_s,
    q_send, q_recv, kv_send, kv_recv, ring_send, ring_recv, o_send, o_recv,
    own_sem, list_sem,
):
    y, z, h = lax.axis_index("segment"), lax.axis_index("seq"), lax.axis_index("head")
    plane = ny * nh
    me = y * nh + h
    rows = BLK // nh
    stripe = BLK // ny
    per = nh // ny
    right, left = lax.rem(z + 1, nz), lax.rem(z + nz - 1, nz)
    half = nz // 2

    own_rows = pl.ds(pl.multiple_of(y * stripe, stripe), stripe)
    own_slots = pl.ds(z * HOLD_BLK, HOLD_BLK)
    own_k = pltpu.make_async_copy(ck.at[:, own_rows, :], pk.at[own_slots], own_sem.at[0])
    own_v = pltpu.make_async_copy(cv.at[:, own_rows, :], pv.at[own_slots], own_sem.at[1])
    get_lists = pltpu.make_async_copy(lists.at[h], lists_s, list_sem)

    barrier = pltpu.get_barrier_semaphore()

    ys = [lax.rem(y + d, ny) for d in range(ny)]
    hs = [lax.rem(h + d, nh) for d in range(nh)]
    peers = [(dy, dh) for dy in range(ny) for dh in range(nh) if dy or dh]
    peers.sort(key=lambda p: -min(p[0], ny - p[0]) - min(p[1], nh - p[1]) // 2)
    for dy, dh in peers:
        pl.semaphore_signal(barrier, inc=1, device_id={"segment": ys[dy], "head": hs[dh]})
    for side in (left, right):
        pl.semaphore_signal(barrier, inc=1, device_id={"seq": side})
    own_k.start()
    own_v.start()
    get_lists.start()
    pl.semaphore_wait(barrier, plane + 1)

    tables = (sk, sv, pk, pv)

    def piece(kind, origin):
        if kind < 2:
            return tables[kind].at[:, origin]
        return tables[kind].at[pl.ds(origin * HOLD_BLK, HOLD_BLK)]

    def steps(kind, way):
        return half if kind % 2 == way else half - 1

    def ring_copy(kind, way, step, src, origin):
        return pltpu.make_async_remote_copy(
            src_ref=src,
            dst_ref=piece(kind, origin),
            send_sem=ring_send.at[kind * 2 + way, step],
            recv_sem=ring_recv.at[kind * 2 + way, step],
            device_id={"seq": left if way else right},
        )

    def origin_at(way, step):
        return lax.rem(z + step, nz) if way else lax.rem(z + nz - step, nz)

    def relay(kind, way, step):
        origin = origin_at(way, step)
        last = steps(kind, way)

        def go():
            wait_bytes(piece(kind, origin), ring_recv.at[kind * 2 + way, step - 1])

        def send():
            ring_copy(kind, way, step, piece(kind, origin), origin).start()

        if isinstance(step, int):
            if step <= last:
                go()
            if step < last:
                send()
        else:
            pl.when(step <= last)(go)
            pl.when(step < last)(send)

    for way in (0, 1):
        for kind, src in ((2, ck), (3, cv)):
            if steps(kind, way) > 0:
                ring_copy(kind, way, 0, src.at[:, own_rows, :], z).start()

    target = lax.div(h, per)
    dst_rows = pl.ds(pl.multiple_of(lax.rem(h, per) * rows, rows), rows)

    def head_cols(i, width):
        return pl.ds(pl.multiple_of(i * width, width), width)

    def send_kv(dh, local_copy):
        for n, (src, tab) in enumerate(((k_in, sk), (v_in, sv))):
            src, dst = src.at[:, head_cols(hs[dh], HD)], tab.at[y, z, dst_rows]
            if local_copy:
                pltpu.make_async_copy(src, dst, kv_recv.at[n]).start()
            else:
                pltpu.make_async_remote_copy(
                    src_ref=src,
                    dst_ref=dst,
                    send_sem=kv_send.at[n],
                    recv_sem=kv_recv.at[n],
                    device_id={"segment": target, "head": hs[dh]},
                ).start()

    for dh in sorted(range(nh), key=lambda d: -min(d, nh - d)):
        if dh:
            send_kv(dh, False)
        else:
            pl.when(target == y)(lambda: send_kv(0, True))
            pl.when(target != y)(lambda: send_kv(0, False))

    def send_queries():
        pltpu.make_async_copy(q_in.at[:, head_cols(h, QPG * HD)], qb.at[me], q_recv).start()
        for dy, dh in peers:
            pltpu.make_async_remote_copy(
                src_ref=q_in.at[:, head_cols(hs[dh], QPG * HD)],
                dst_ref=qb.at[me],
                send_sem=q_send,
                recv_sem=q_recv,
                device_id={"segment": ys[dy], "head": hs[dh]},
            ).start()

    acc[...] = jnp.zeros_like(acc)
    peak[...] = jnp.full(peak.shape, -1e30, jnp.float32)

    def ring_step(s, kinds):
        for kind in kinds:
            for way in (0, 1):
                relay(kind, way, s)

    for n, tab in enumerate((sk, sv)):
        wait_bytes(tab.at[:, z], kv_recv.at[n])
        for way in (0, 1):
            if steps(n, way) > 0:
                ring_copy(n, way, 0, piece(n, z), z).start()
    ring_step(1, (2, 3))
    send_queries()
    ring_step(1, (0, 1))

    def queries_of(yp, group):
        parts = [
            qb[pl.ds(yp * nh, nh), :, head_cols(group * GROUP + j, HD)].reshape(BLK, HD)
            for j in range(GROUP)
        ]
        return jnp.concatenate(parts, axis=0)

    def fold(yp, group, keys, values, mask, keep):
        s = lax.dot_general(queries_of(yp, group), keys, NT, preferred_element_type=jnp.float32)
        if mask is not None:
            n = s.shape[1] - mask.shape[1]
            tail = s[:, n:] + jnp.concatenate([mask] * GROUP, axis=0)
            s = jnp.concatenate([s[:, :n], tail], axis=1) if n else tail
        values = jnp.concatenate([values, jnp.ones_like(values)], axis=1)
        heads = pl.ds(yp * QPG + group * GROUP, GROUP)
        m1 = peak[heads].reshape(GROUP * BLK, HD)
        m = jnp.maximum(m1, jnp.max(s, axis=1, keepdims=True) * SCALE)
        mm = jnp.concatenate([m] * (s.shape[1] // HD), axis=1)
        w = jnp.exp2(s * SCALE - mm).astype(jnp.bfloat16)
        r = lax.dot_general(w, values, NN, preferred_element_type=jnp.float32)
        fade = jnp.exp2(m1 - m)
        fade = jnp.concatenate([fade, fade], axis=1)
        a = acc[heads].reshape(GROUP * BLK, 2 * HD) * fade + r
        if keep:
            acc[heads] = a.reshape(GROUP, BLK, 2 * HD)
            peak[heads] = m.reshape(GROUP, BLK, HD)
        return m, a

    def take_chunk(chunk):
        places = [
            lax.rem(z + 2 * chunk, nz),
            lax.rem(z + nz - 2 * chunk - 1, nz),
            lax.rem(z + 2 * chunk + 1, nz),
            lax.rem(z + nz - 2 * chunk - 2, nz),
        ]
        row = lax.broadcasted_iota(jnp.int32, (BLK, 4 * stripe), 0)
        col = lax.broadcasted_iota(jnp.int32, (BLK, 4 * stripe), 1)
        key_pos = lax.rem(col, stripe) + y * stripe
        for i, place in enumerate(places):
            key_pos = key_pos + jnp.where(lax.div(col, stripe) == i, place * BLK, 0)
            for yp in range(ny):
                rows_i = slice(i * stripe, (i + 1) * stripe)
                kc[yp, rows_i, :] = sk[yp, place]
                vc[yp, rows_i, :] = sv[yp, place]
        bias[...] = jnp.where(key_pos <= z * BLK + row, 0.0, -1e30).astype(jnp.float32)

    def span_half(t):
        pl.when(lax.rem(t, 2) == 0)(lambda: take_chunk(lax.div(t, 2)))
        for yp in range(ny):
            n = (yp + 1) * 4 * stripe
            keys = kc[0 : yp + 1].reshape(n, HD)
            values = vc[0 : yp + 1].reshape(n, HD)
            fold(yp, lax.rem(t, 2), keys, values, bias[...], True)

    chunks = half // 2 - 1
    first = half - chunks

    def step_body(s, _):
        ring_step(s, (2, 3))
        pl.when(s == first)(functools.partial(wait_bytes, qb, q_recv))
        at = 2 * (s - first)
        pl.when(s >= first)(lambda: span_half(at))
        ring_step(s, (0, 1))
        pl.when(s >= first)(lambda: span_half(at + 1))
        return 0

    lax.fori_loop(2, half, step_body, 0)
    ring_step(half, (2, 3))
    if chunks == 0:
        wait_bytes(qb, q_recv)
    own_k.wait()
    own_v.wait()
    get_lists.wait()

    def prefix(yp):
        for i in range(SEL):
            block = lists_s[i, yp * nz + z]
            at = hold[block] * HOLD_BLK + slot[block]
            kp[i * stripe : (i + 1) * stripe, :] = pk[at]
            vp[i * stripe : (i + 1) * stripe, :] = pv[at]
        for group in range(QPG // GROUP):
            fold(yp, group, kp[...], vp[...], None, True)

    lane = lax.broadcasted_iota(jnp.int32, (BLK, HD), 1)
    order = sorted(range(ny), key=lambda o: (o == 0, -min(o, ny - o)))
    for o in order:
        yp = ys[o]
        prefix(yp)
        if o == order[0]:
            ring_step(half, (0, 1))
            take_chunk(half // 2 - 1)
        keys = kc[...].reshape(ny * 4 * stripe, HD)
        values = vc[...].reshape(ny * 4 * stripe, HD)
        mask = jnp.concatenate(
            [
                jnp.where(jnp.full(bias.shape, i, jnp.int32) < yp, 0.0, bias[...])
                + jnp.where(jnp.full(bias.shape, i, jnp.int32) > yp, -1e30, 0.0)
                for i in range(ny)
            ],
            axis=1,
        )
        for group in range(QPG // GROUP):
            m, a = fold(yp, group, keys, values, mask, False)
            total = a[:, HD:]
            mixed = (a[:, :HD] / total).astype(jnp.bfloat16)
            lse = m + jnp.log2(total)
            level = jnp.zeros((BLK, HD), jnp.float32)
            for j in range(GROUP):
                rows_j = slice(j * BLK, (j + 1) * BLK)
                cols = slice((group * GROUP + j) * HD, (group * GROUP + j + 1) * HD)
                sendo[yp, :, cols] = mixed[rows_j]
                level = jnp.where(lane == j, lse[rows_j], level)
            sendl[yp, group] = level.T[:8]
            if o:
                cols = slice(group * GROUP * HD, (group + 1) * GROUP * HD)
                for n, (src, dst) in enumerate(
                    (
                        (sendl.at[yp, group], recvl.at[y, group]),
                        (sendo.at[yp, :, cols], recvo.at[y, :, cols]),
                    )
                ):
                    pltpu.make_async_remote_copy(
                        src_ref=src,
                        dst_ref=dst,
                        send_sem=o_send.at[n, o, group],
                        recv_sem=o_recv.at[n, o, group],
                        device_id={"segment": yp},
                    ).start()

    fill = jnp.zeros((BLK - 8, BLK), jnp.float32)
    for group in range(QPG // GROUP):
        cols = slice(group * GROUP * HD, (group + 1) * GROUP * HD)
        levels = [sendl[y, group]]
        parts = [sendo.at[y]]
        for o in order[:-1]:
            src = lax.rem(y + ny - o, ny)
            wait_bytes(recvl.at[src, group], o_recv.at[0, o, group])
            wait_bytes(recvo.at[src, :, cols], o_recv.at[1, o, group])
            levels.append(recvl[src, group])
            parts.append(recvo.at[src])
        top = functools.reduce(jnp.maximum, levels)
        shares = [jnp.exp2(v - top) for v in levels]
        norm = 1.0 / functools.reduce(jnp.add, shares)
        shares = [jnp.concatenate([v * norm, fill], axis=0).T for v in shares]
        for j in range(GROUP):
            cols = slice((group * GROUP + j) * HD, (group * GROUP + j + 1) * HD)
            out[:, cols] = functools.reduce(
                jnp.add,
                [
                    w[:, j : j + 1] * part[:, cols].astype(jnp.float32)
                    for w, part in zip(shares, parts)
                ],
            ).astype(jnp.bfloat16)

    wait_bytes(qb.at[: plane - 1], q_send)
    for n, src in enumerate((k_in, v_in)):
        pl.when(target == y)(
            functools.partial(wait_bytes, src.at[:, : (nh - 1) * HD], kv_send.at[n])
        )
        pl.when(target != y)(functools.partial(wait_bytes, src, kv_send.at[n]))
    for kind in range(4):
        for way in (0, 1):
            count = steps(kind, way)

            def sent(step, _, kind=kind, way=way):
                wait_bytes(piece(kind, z), ring_send.at[kind * 2 + way, step])
                return 0

            lax.fori_loop(0, count, sent, 0)
    for o in range(1, ny):
        for group in range(QPG // GROUP):
            wait_bytes(sendl.at[0, group], o_send.at[0, o, group])
            wait_bytes(sendo.at[0, :, : GROUP * HD], o_send.at[1, o, group])


def local(ny, nz, nh, q, k, v, ck, cv, hold, slot, lists):
    rows, width, stripe = BLK // nh, QPG * HD, BLK // ny
    blocks = ck.shape[0] * nz
    ck = ck.reshape(ck.shape[0], BLK, HD)
    cv = cv.reshape(cv.shape[0], BLK, HD)
    lists = jnp.transpose(lists, (1, 2, 0))
    hbm, smem = pl.BlockSpec(memory_space=pltpu.HBM), pl.BlockSpec(memory_space=pltpu.SMEM)
    bf, f32, dma = jnp.bfloat16, jnp.float32, pltpu.SemaphoreType.DMA
    return pl.pallas_call(
        functools.partial(kernel, ny, nz, nh),
        out_shape=jax.ShapeDtypeStruct((BLK, width), bf),
        in_specs=[hbm] * 5 + [smem, smem, hbm],
        out_specs=pl.BlockSpec(memory_space=pltpu.VMEM),
        scratch_shapes=[
            pltpu.VMEM((ny * nh, rows, width), bf),
            pltpu.VMEM((ny, nz, stripe, HD), bf),
            pltpu.VMEM((ny, nz, stripe, HD), bf),
            pltpu.VMEM((blocks, stripe, HD), bf),
            pltpu.VMEM((blocks, stripe, HD), bf),
            pltpu.VMEM((ny, 4 * stripe, HD), bf),
            pltpu.VMEM((ny, 4 * stripe, HD), bf),
            pltpu.VMEM((BLK, 4 * stripe), f32),
            pltpu.VMEM((ny * QPG, BLK, 2 * HD), f32),
            pltpu.VMEM((ny * QPG, BLK, HD), f32),
            pltpu.VMEM((ny, BLK, width), bf),
            pltpu.VMEM((ny, BLK, width), bf),
            pltpu.VMEM((ny, QPG // GROUP, 8, BLK), f32),
            pltpu.VMEM((ny, QPG // GROUP, 8, BLK), f32),
            pltpu.VMEM((SEL * stripe, HD), bf),
            pltpu.VMEM((SEL * stripe, HD), bf),
            pltpu.SMEM((SEL, lists.shape[2]), jnp.int32),
            dma, dma, dma((2,)), dma((2,)),
            dma((8, nz // 2)), dma((8, nz // 2)),
            dma((2, ny, QPG // GROUP)), dma((2, ny, QPG // GROUP)),
            dma((2,)), dma,
        ],
        compiler_params=pltpu.CompilerParams(
            collective_id=0, has_side_effects=True, vmem_limit_bytes=60 * 2**20
        ),
        cost_estimate=pl.CostEstimate(
            flops=4 * BLK * QPG * HD * 6144, bytes_accessed=2**24, transcendentals=6144 * 1024
        ),
        name="attend",
    )(q, k, v, ck, cv, hold, slot, lists)


def solution(mesh):
    ny, nz, nh = mesh.shape["segment"], mesh.shape["seq"], mesh.shape["head"]
    placed = (
        P(("segment", "seq", "head"), None),
        P(("segment", "seq", "head"), None),
        P(("segment", "seq", "head"), None),
        P("seq", None, "head", None),
        P("seq", None, "head", None),
        P(),
        P(),
        P(),
    )
    return jax.shard_map(
        functools.partial(local, ny, nz, nh),
        mesh=mesh,
        in_specs=placed,
        out_specs=P(("segment", "seq"), "head"),
        check_vma=False,
    )
```

time: 96.1 us -> 71.2 us (0.74)
  the two profiles are of different devices: /device:TPU:34 before, /device:TPU:1 now
where the time goes in v2:
time: 71.2 us; the launch traced here: 71 us
  Pallas kernels  69.3 us (97%)
  local copies, waits for them, and re-layouts  1.67 us (2%)
    pallas_call x1, Pallas kernels, local(): pl.pallas_call(functools.partial(kernel, ny, nz, nh), out_shape=jax.Shape...  69.3 us
    unnamed x1, local copies, waits for them, and re-layouts  1.67 us

profile of v2, /device:TPU:1, one launch (start us, length us, event | category | flops | bytes accessed | tf_op | source)
XLA Modules:
  0.0 71.0 jit_solution(9489449903392793629)
XLA Ops:
  0.0 69.3 %attend.1 = bf16[128,1024]{1,0:T(8,128)(2,1)} custom-call(bf16[16,8192]{1,0:T(8,128)(2,1)} %q_in.1, bf16[16,1024]{1,0:T(8,128)(2,1)} %k_in.1, bf16[16,1024]{1,0:T(8,128)(2,1)} %v_in.1, bf16[8,128,128]{2,1,0:T(8,128)(2,1)} %bitcast.3, bf16[8,128,128]{2,1,0:T(8,128)(2,1)} %bitcast.4, s32[128]{0:T(128)} %hold.1, s32[128]{0:T(128)} %slot.1, s32[8,8,64]{2,1,0:T(8,128)} %bitcast.5), custom_call_target="tpu_custom_call" | custom-call | flops 3221225472 | bytes 16777216 | tf_op jit(solution)/shard_map/attend/pallas_call | solution.py:347
  69.4 1.7 %copy.10 = bf16[128,1024]{1,0:T(8,128)(2,1)} copy(bf16[128,1024]{1,0:T(8,128)(2,1)} %attend.1) | data formatting | bytes 524288

commit v3 on v2

--- a/solution.py
+++ b/solution.py
@@ -25,8 +25,8 @@
 
 def kernel(
     ny, nz, nh,
-    q_in, k_in, v_in, ck, cv, hold, slot, lists, out,
-    qb, sk, sv, pk, pv, kc, vc, bias, acc, peak, sendo, recvo, sendl, recvl, kp, vp, lists_s,
+    q_in, k_in, v_in, ck, cv, hold_in, slot_in, lists, out,
+    qb, sk, sv, pk, pv, kc, vc, bias, acc, peak, sendo, recvo, sendl, recvl, kp, vp, lists_s, hold, slot,
     q_send, q_recv, kv_send, kv_recv, ring_send, ring_recv, o_send, o_recv,
     own_sem, list_sem,
 ):
@@ -43,7 +43,10 @@
     own_slots = pl.ds(z * HOLD_BLK, HOLD_BLK)
     own_k = pltpu.make_async_copy(ck.at[:, own_rows, :], pk.at[own_slots], own_sem.at[0])
     own_v = pltpu.make_async_copy(cv.at[:, own_rows, :], pv.at[own_slots], own_sem.at[1])
-    get_lists = pltpu.make_async_copy(lists.at[h], lists_s, list_sem)
+    indices = [
+        pltpu.make_async_copy(src, dst, list_sem.at[n])
+        for n, (src, dst) in enumerate(((lists.at[h], lists_s), (hold_in, hold), (slot_in, slot)))
+    ]
 
     barrier = pltpu.get_barrier_semaphore()
 
@@ -57,7 +60,8 @@
         pl.semaphore_signal(barrier, inc=1, device_id={"seq": side})
     own_k.start()
     own_v.start()
-    get_lists.start()
+    for copy in indices:
+        copy.start()
     pl.semaphore_wait(barrier, plane + 1)
 
     tables = (sk, sv, pk, pv)
@@ -144,9 +148,6 @@
                 device_id={"segment": ys[dy], "head": hs[dh]},
             ).start()
 
-    acc[...] = jnp.zeros_like(acc)
-    peak[...] = jnp.full(peak.shape, -1e30, jnp.float32)
-
     def ring_step(s, kinds):
         for kind in kinds:
             for way in (0, 1):
@@ -160,6 +161,8 @@
     ring_step(1, (2, 3))
     send_queries()
     ring_step(1, (0, 1))
+    acc[...] = jnp.zeros_like(acc)
+    peak[...] = jnp.full(peak.shape, -1e30, jnp.float32)
 
     def queries_of(yp, group):
         parts = [
@@ -219,11 +222,11 @@
     first = half - chunks
 
     def step_body(s, _):
-        ring_step(s, (2, 3))
+        ring_step(s, (2, 0))
         pl.when(s == first)(functools.partial(wait_bytes, qb, q_recv))
         at = 2 * (s - first)
         pl.when(s >= first)(lambda: span_half(at))
-        ring_step(s, (0, 1))
+        ring_step(s, (3, 1))
         pl.when(s >= first)(lambda: span_half(at + 1))
         return 0
 
@@ -233,7 +236,8 @@
         wait_bytes(qb, q_recv)
     own_k.wait()
     own_v.wait()
-    get_lists.wait()
+    for copy in indices:
+        copy.wait()
 
     def prefix(yp):
         for i in range(SEL):
@@ -342,12 +346,12 @@
     ck = ck.reshape(ck.shape[0], BLK, HD)
     cv = cv.reshape(cv.shape[0], BLK, HD)
     lists = jnp.transpose(lists, (1, 2, 0))
-    hbm, smem = pl.BlockSpec(memory_space=pltpu.HBM), pl.BlockSpec(memory_space=pltpu.SMEM)
+    hbm = pl.BlockSpec(memory_space=pltpu.HBM)
     bf, f32, dma = jnp.bfloat16, jnp.float32, pltpu.SemaphoreType.DMA
     return pl.pallas_call(
         functools.partial(kernel, ny, nz, nh),
         out_shape=jax.ShapeDtypeStruct((BLK, width), bf),
-        in_specs=[hbm] * 5 + [smem, smem, hbm],
+        in_specs=[hbm] * 8,
         out_specs=pl.BlockSpec(memory_space=pltpu.VMEM),
         scratch_shapes=[
             pltpu.VMEM((ny * nh, rows, width), bf),
@@ -367,10 +371,12 @@
             pltpu.VMEM((SEL * stripe, HD), bf),
             pltpu.VMEM((SEL * stripe, HD), bf),
             pltpu.SMEM((SEL, lists.shape[2]), jnp.int32),
+            pltpu.SMEM(hold.shape, jnp.int32),
+            pltpu.SMEM(slot.shape, jnp.int32),
             dma, dma, dma((2,)), dma((2,)),
             dma((8, nz // 2)), dma((8, nz // 2)),
             dma((2, ny, QPG // GROUP)), dma((2, ny, QPG // GROUP)),
-            dma((2,)), dma,
+            dma((2,)), dma((3,)),
         ],
         compiler_params=pltpu.CompilerParams(
             collective_id=0, has_side_effects=True, vmem_limit_bytes=60 * 2**20

time: 71.2 us -> 68.4 us (0.961)
  Pallas kernels: 69.3 us -> 66.1 us
    pallas_call x1, Pallas kernels: 69.3 us -> 66.1 us  [local(): pl.pallas_call(functools.partial(kernel, ny, nz, nh), out_shape=jax.Shape...]
where the time goes in v3:
time: 68.4 us; the launch traced here: 67.8 us
  Pallas kernels  66.1 us (97%)
  local copies, waits for them, and re-layouts  1.67 us (2%)
    pallas_call x1, Pallas kernels, local(): pl.pallas_call(functools.partial(kernel, ny, nz, nh), out_shape=jax.Shape...  66.1 us
    unnamed x1, local copies, waits for them, and re-layouts  1.67 us

profile of v3, /device:TPU:1, one launch (start us, length us, event | category | flops | bytes accessed | tf_op | source)
XLA Modules:
  0.0 67.8 jit_solution(15425450700805397020)
XLA Ops:
  0.0 66.1 %attend.1 = bf16[128,1024]{1,0:T(8,128)(2,1)} custom-call(bf16[16,8192]{1,0:T(8,128)(2,1)} %q_in.1, bf16[16,1024]{1,0:T(8,128)(2,1)} %k_in.1, bf16[16,1024]{1,0:T(8,128)(2,1)} %v_in.1, bf16[8,128,128]{2,1,0:T(8,128)(2,1)} %bitcast.3, bf16[8,128,128]{2,1,0:T(8,128)(2,1)} %bitcast.4, s32[128]{0:T(128)} %hold_in.1, s32[128]{0:T(128)} %slot_in.1, ...), custom_call_target="tpu_custom_call" | custom-call | flops 3221225472 | bytes 16777216 | tf_op jit(solution)/shard_map/attend/pallas_call | solution.py:351
  66.1 1.7 %copy.10 = bf16[128,1024]{1,0:T(8,128)(2,1)} copy(bf16[128,1024]{1,0:T(8,128)(2,1)} %attend.1) | data formatting | bytes 524288

commit v4 on v3

--- a/solution.py
+++ b/solution.py
@@ -159,8 +159,8 @@
             if steps(n, way) > 0:
                 ring_copy(n, way, 0, piece(n, z), z).start()
     ring_step(1, (2, 3))
+    ring_step(1, (0, 1))
     send_queries()
-    ring_step(1, (0, 1))
     acc[...] = jnp.zeros_like(acc)
     peak[...] = jnp.full(peak.shape, -1e30, jnp.float32)
 
@@ -210,24 +210,28 @@
                 vc[yp, rows_i, :] = sv[yp, place]
         bias[...] = jnp.where(key_pos <= z * BLK + row, 0.0, -1e30).astype(jnp.float32)
 
-    def span_half(t):
-        pl.when(lax.rem(t, 2) == 0)(lambda: take_chunk(lax.div(t, 2)))
-        for yp in range(ny):
+    def span_part(t, blocks):
+        for yp in blocks:
             n = (yp + 1) * 4 * stripe
             keys = kc[0 : yp + 1].reshape(n, HD)
             values = vc[0 : yp + 1].reshape(n, HD)
-            fold(yp, lax.rem(t, 2), keys, values, bias[...], True)
+            fold(yp, t, keys, values, bias[...], True)
 
     chunks = half // 2 - 1
     first = half - chunks
 
     def step_body(s, _):
-        ring_step(s, (2, 0))
+        late = s >= first
+        ring_step(s, (2,))
         pl.when(s == first)(functools.partial(wait_bytes, qb, q_recv))
-        at = 2 * (s - first)
-        pl.when(s >= first)(lambda: span_half(at))
-        ring_step(s, (3, 1))
-        pl.when(s >= first)(lambda: span_half(at + 1))
+        pl.when(late)(lambda: take_chunk(s - first))
+        pl.when(late)(lambda: span_part(0, range(ny - 1, ny)))
+        ring_step(s, (0,))
+        pl.when(late)(lambda: span_part(0, range(ny - 1)))
+        ring_step(s, (3,))
+        pl.when(late)(lambda: span_part(1, range(ny - 1, ny)))
+        ring_step(s, (1,))
+        pl.when(late)(lambda: span_part(1, range(ny - 1)))
         return 0
 
     lax.fori_loop(2, half, step_body, 0)

time: 68.4 us -> 68.4 us (level)
  no operation moved by 1% of the time
where the time goes in v4:
time: 68.4 us; the launch traced here: 67.8 us
  Pallas kernels  66.1 us (97%)
  local copies, waits for them, and re-layouts  1.67 us (2%)
    pallas_call x1, Pallas kernels, local(): pl.pallas_call(functools.partial(kernel, ny, nz, nh), out_shape=jax.Shape...  66.1 us
    unnamed x1, local copies, waits for them, and re-layouts  1.67 us

profile of v4, /device:TPU:1, one launch (start us, length us, event | category | flops | bytes accessed | tf_op | source)
XLA Modules:
  0.0 67.8 jit_solution(2068018876256029858)
XLA Ops:
  0.0 66.1 %attend.1 = bf16[128,1024]{1,0:T(8,128)(2,1)} custom-call(bf16[16,8192]{1,0:T(8,128)(2,1)} %q_in.1, bf16[16,1024]{1,0:T(8,128)(2,1)} %k_in.1, bf16[16,1024]{1,0:T(8,128)(2,1)} %v_in.1, bf16[8,128,128]{2,1,0:T(8,128)(2,1)} %bitcast.3, bf16[8,128,128]{2,1,0:T(8,128)(2,1)} %bitcast.4, s32[128]{0:T(128)} %hold_in.1, s32[128]{0:T(128)} %slot_in.1, ...), custom_call_target="tpu_custom_call" | custom-call | flops 3221225472 | bytes 16777216 | tf_op jit(solution)/shard_map/attend/pallas_call | solution.py:355
  66.1 1.7 %copy.10 = bf16[128,1024]{1,0:T(8,128)(2,1)} copy(bf16[128,1024]{1,0:T(8,128)(2,1)} %attend.1) | data formatting | bytes 524288
